TPU v7x, 256 devices: a whole 4x4x8 slice. The times are simulated.
256 devices in a mesh: tok: 32 (over x, z), head: 8 (over y, core).
Axes of the slice: x: 4, y: 4, z: 8, core: 2. Of those that a mesh axis runs over, the one named last changes fastest.
Arguments:
- queries: bfloat16 [32768, 4096], P(('tok', 'head')), may hold values from -6 to 6
- key_tokens: bfloat16 [32768, 4096], P(('tok', 'head')), may hold values from -6 to 6
- values: bfloat16 [32768, 4096], P(('tok', 'head')), may hold values from -6 to 6
- out_grad: bfloat16 [32768, 4096], P(('tok', 'head')), may hold values from -6 to 6
- learn_rates: float32 [32768, 16], P('tok', 'head'), may hold values from 0.2 to 2
- w_gate: bfloat16 [16, 256, 256], P('head'), may hold values from -0.375 to 0.375
- w_up: bfloat16 [16, 256, 256], P('head'), may hold values from -0.375 to 0.375
- w_down: bfloat16 [16, 256, 256], P('head'), may hold values from -0.375 to 0.375
Outputs:
- grad_queries: bfloat16 [32768, 4096], P(('tok', 'head'))
- grad_keys: bfloat16 [32768, 4096], P(('tok', 'head'))
- grad_values: bfloat16 [32768, 4096], P(('tok', 'head'))
All inputs are finite; a program needn't handle non-finite values.
Results may differ from a plain program's by a relative error of at most 0.02.
Values may be sent and summed in bfloat16 or wider, within the bound.
A program may use at most 128 MiB of HBM per device.

v0:
```python
import math

import jax
import jax.numpy as jnp
from jax import lax
from jax.sharding import PartitionSpec as P

DH = 256


def silu_slope(pre_act):
    sigmoid_val = jax.nn.sigmoid(pre_act)
    return sigmoid_val * (1.0 + pre_act * (1.0 - sigmoid_val))


def silu_curve(pre_act):
    sigmoid_val = jax.nn.sigmoid(pre_act)
    return sigmoid_val * (1.0 - sigmoid_val) * (2.0 + pre_act * (1.0 - 2.0 * sigmoid_val))


def key_forward(key_rows, scaled, gate_mat, up_mat, down_mat):
    gate_pre = jnp.dot(key_rows, gate_mat, preferred_element_type=jnp.float32)
    up_pre = jnp.dot(key_rows, up_mat, preferred_element_type=jnp.float32)
    gate_act = jax.nn.silu(gate_pre)
    hidden = (gate_act * up_pre).astype(jnp.bfloat16)
    key_dhid = jnp.dot(scaled, down_mat.T, preferred_element_type=jnp.float32)
    grad_gate = (key_dhid * up_pre * silu_slope(gate_pre)).astype(jnp.bfloat16)
    grad_upper = (key_dhid * gate_act).astype(jnp.bfloat16)
    delta_gate = jnp.dot(key_rows.T, grad_gate, preferred_element_type=jnp.float32)
    delta_up = jnp.dot(key_rows.T, grad_upper, preferred_element_type=jnp.float32)
    delta_down = jnp.dot(hidden.T, scaled, preferred_element_type=jnp.float32)
    stored = (gate_pre, up_pre, hidden, key_dhid, grad_gate, grad_upper)
    return ((delta_gate, delta_up, delta_down), stored)


def query_side(query_rows, out_rows, fresh_gate, fresh_up, fresh_down):
    gate_pre = jnp.dot(query_rows, fresh_gate, preferred_element_type=jnp.float32)
    up_pre = jnp.dot(query_rows, fresh_up, preferred_element_type=jnp.float32)
    gate_act = jax.nn.silu(gate_pre)
    hidden = (gate_act * up_pre).astype(jnp.bfloat16)
    query_dhid = jnp.dot(out_rows, fresh_down.T, preferred_element_type=jnp.float32)
    grad_gate = (query_dhid * up_pre * silu_slope(gate_pre)).astype(jnp.bfloat16)
    grad_upper = (query_dhid * gate_act).astype(jnp.bfloat16)
    query_grad = jnp.dot(grad_gate, fresh_gate.T, preferred_element_type=jnp.float32)
    query_grad = query_grad + jnp.dot(grad_upper, fresh_up.T, preferred_element_type=jnp.float32)
    sum_gate = jnp.dot(query_rows.T, grad_gate, preferred_element_type=jnp.float32)
    sum_up = jnp.dot(query_rows.T, grad_upper, preferred_element_type=jnp.float32)
    sum_down = jnp.dot(hidden.T, out_rows, preferred_element_type=jnp.float32)
    return (query_grad.astype(jnp.bfloat16), (sum_gate, sum_up, sum_down))


def key_back(
    key_rows, scaled, rate_col, gate_mat, up_mat, down_mat, stored, adj_gate, adj_up, adj_down
):
    gate_pre, up_pre, hidden, key_dhid, grad_gate, grad_upper = stored
    back_dgate = jnp.dot(key_rows, adj_gate, preferred_element_type=jnp.float32)
    back_dup = jnp.dot(key_rows, adj_up, preferred_element_type=jnp.float32)
    back_hidden = jnp.dot(scaled, adj_down.T, preferred_element_type=jnp.float32)
    back_scaled = jnp.dot(hidden, adj_down, preferred_element_type=jnp.float32)
    gate_act = jax.nn.silu(gate_pre)
    gate_slope = silu_slope(gate_pre)
    back_dhid = (back_dgate * up_pre * gate_slope + back_dup * gate_act).astype(jnp.bfloat16)
    back_gate = (
        back_dgate * key_dhid * up_pre * silu_curve(gate_pre)
        + (back_dup * key_dhid + back_hidden * up_pre) * gate_slope
    ).astype(jnp.bfloat16)
    back_upper = (back_dgate * key_dhid * gate_slope + back_hidden * gate_act).astype(jnp.bfloat16)
    key_grad = jnp.dot(grad_gate, adj_gate.T, preferred_element_type=jnp.float32)
    key_grad = key_grad + jnp.dot(grad_upper, adj_up.T, preferred_element_type=jnp.float32)
    key_grad = key_grad + jnp.dot(back_gate, gate_mat.T, preferred_element_type=jnp.float32)
    key_grad = key_grad + jnp.dot(back_upper, up_mat.T, preferred_element_type=jnp.float32)
    value_grad = rate_col[:, None] * (
        back_scaled + jnp.dot(back_dhid, down_mat, preferred_element_type=jnp.float32)
    )
    return (key_grad.astype(jnp.bfloat16), value_grad.astype(jnp.bfloat16))


def body(queries, key_tokens, values, out_grad, learn_rates, w_gate, w_up, w_down):
    query_all, key_all, value_all, out_all = (
        lax.all_to_all(queries, "head", split_axis=1, concat_axis=0, tiled=True),
        lax.all_to_all(key_tokens, "head", split_axis=1, concat_axis=0, tiled=True),
        lax.all_to_all(values, "head", split_axis=1, concat_axis=0, tiled=True),
        lax.all_to_all(out_grad, "head", split_axis=1, concat_axis=0, tiled=True),
    )
    local_heads = w_gate.shape[0]
    local_rows = query_all.shape[0]
    update_scale = 1.0 / math.sqrt(DH * local_rows * lax.axis_size("tok"))

    def by_head(matrix):
        return matrix.reshape(local_rows, local_heads, DH)

    scaled = (learn_rates[:, :, None] * by_head(value_all).astype(jnp.float32)).astype(jnp.bfloat16)
    key_heads = by_head(key_all)
    deltas, stored = jax.vmap(key_forward, in_axes=(1, 1, 0, 0, 0))(
        key_heads, scaled, w_gate, w_up, w_down
    )
    delta_gate, delta_up, delta_down = deltas
    total_gate, total_up, total_down = lax.psum((delta_gate, delta_up, delta_down), "tok")
    fresh_gate = (w_gate.astype(jnp.float32) + update_scale * total_gate).astype(jnp.bfloat16)
    fresh_up = (w_up.astype(jnp.float32) + update_scale * total_up).astype(jnp.bfloat16)
    fresh_down = (w_down.astype(jnp.float32) + update_scale * total_down).astype(jnp.bfloat16)
    query_grad, sums = jax.vmap(query_side, in_axes=(1, 1, 0, 0, 0), out_axes=(1, 0))(
        by_head(query_all), by_head(out_all), fresh_gate, fresh_up, fresh_down
    )
    query_flat = query_grad.reshape(local_rows, local_heads * DH)
    sum_gate, sum_up, sum_down = (
        lax.psum(sums[0].astype(jnp.bfloat16), "tok").astype(jnp.float32),
        lax.psum(sums[1].astype(jnp.bfloat16), "tok").astype(jnp.float32),
        lax.psum(sums[2].astype(jnp.bfloat16), "tok").astype(jnp.float32),
    )
    adj_gate = (update_scale * sum_gate).astype(jnp.bfloat16)
    adj_up = (update_scale * sum_up).astype(jnp.bfloat16)
    adj_down = (update_scale * sum_down).astype(jnp.bfloat16)
    key_grad, value_grad = jax.vmap(
        key_back, in_axes=(1, 1, 1, 0, 0, 0, 0, 0, 0, 0), out_axes=(1, 1)
    )(key_heads, scaled, learn_rates, w_gate, w_up, w_down, stored, adj_gate, adj_up, adj_down)
    key_flat = key_grad.reshape(local_rows, local_heads * DH)
    value_flat = value_grad.reshape(local_rows, local_heads * DH)
    query_home, key_home, value_home = (
        lax.all_to_all(query_flat, "head", split_axis=0, concat_axis=1, tiled=True),
        lax.all_to_all(key_flat, "head", split_axis=0, concat_axis=1, tiled=True),
        lax.all_to_all(value_flat, "head", split_axis=0, concat_axis=1, tiled=True),
    )
    return (query_home, key_home, value_home)


def solution(mesh):
    return jax.shard_map(
        body,
        mesh=mesh,
        in_specs=(
            P(("tok", "head"), None),
            P(("tok", "head"), None),
            P(("tok", "head"), None),
            P(("tok", "head"), None),
            P("tok", "head"),
            P("head", None, None),
            P("head", None, None),
            P("head", None, None),
        ),
        out_specs=(P(("tok", "head"), None), P(("tok", "head"), None), P(("tok", "head"), None)),
        check_vma=False,
    )
```

profile of v0, /device:TPU:1, one launch (start us, length us, event | category | flops | bytes accessed | tf_op | source)
XLA Modules:
  0.0 452.2 jit_solution(11478676873263375314)
XLA Ops:
  7.2 2.4 copy.114
  9.5 6.7 %all-to-all-start = ((bf16[128,8,512]{0,2,1:T(8,128)(2,1)}), bf16[128,8,512]{0,2,1:T(8,128)(2,1)S(1)}, u32[]{:S(2)}, u32[]{:S(2)}) async-start(bf16[128,8,512]{0,2,1:T(8,128)(2,1)} %bitcast), calls=%async_computation | async-start | bytes 2097152 | tf_op jit(solution)/shard_map/all_to_all | solution.py:81
  17.5 13.8 %all-to-all-done = bf16[128,8,512]{0,2,1:T(8,128)(2,1)S(1)} async-done(((bf16[128,8,512]{0,2,1:T(8,128)(2,1)}), bf16[128,8,512]{0,2,1:T(8,128)(2,1)S(1)}, u32[]{:S(2)}, u32[]{:S(2)}) %all-to-all-start) | async-done | bytes 1048608 | tf_op jit(solution)/shard_map/all_to_all | solution.py:81
  31.3 4.3 all-to-all-start.1
  38.2 12.6 %all-to-all-done.1 = bf16[128,8,512]{0,2,1:T(8,128)(2,1)S(1)} async-done(((bf16[128,8,512]{0,2,1:T(8,128)(2,1)}), bf16[128,8,512]{0,2,1:T(8,128)(2,1)S(1)}, u32[]{:S(2)}, u32[]{:S(2)}) %all-to-all-start.1) | async-done | bytes 1048608 | tf_op jit(solution)/shard_map/all_to_all | solution.py:82
  50.8 5.0 %all-to-all-start.3 = ((bf16[128,8,512]{0,2,1:T(8,128)(2,1)}), bf16[128,8,512]{0,2,1:T(8,128)(2,1)}, u32[]{:S(2)}, u32[]{:S(2)}) async-start(bf16[128,8,512]{0,2,1:T(8,128)(2,1)} %bitcast.9), calls=%async_computation.3 | async-start | bytes 2097152 | tf_op jit(solution)/shard_map/all_to_all | solution.py:80
  58.7 2.9 copy.120
  61.6 2.0 multiply_convert_fusion.2
  65.7 2.7 multiply_convert_fusion.3
  68.4 1.7 fusion.61
  74.0 4.8 %all-to-all-start.2 = ((bf16[128,8,512]{0,2,1:T(8,128)(2,1)}), bf16[128,8,512]{0,2,1:T(8,128)(2,1)}, u32[]{:S(2)}, u32[]{:S(2)}) async-start(bf16[128,8,512]{0,2,1:T(8,128)(2,1)} %bitcast.4), calls=%async_computation.2 | async-start | bytes 2097152 | tf_op jit(solution)/shard_map/all_to_all | solution.py:83
  78.8 2.9 copy.129
  83.2 10.8 %all-to-all-done.2 = bf16[128,8,512]{0,2,1:T(8,128)(2,1)} async-done(((bf16[128,8,512]{0,2,1:T(8,128)(2,1)}), bf16[128,8,512]{0,2,1:T(8,128)(2,1)}, u32[]{:S(2)}, u32[]{:S(2)}) %all-to-all-start.2) | async-done | bytes 1048608 | tf_op jit(solution)/shard_map/all_to_all | solution.py:83
  94.1 2.9 copy.123
  96.9 2.3 reshape.52
  99.2 123.5 %all-reduce.5.cloned.1.call-done = (f32[2,256,256]{2,1,0:T(8,128)}, f32[2,256,256]{2,1,0:T(8,128)}, f32[2,256,256]{2,1,0:T(8,128)}) async-done(((f32[2,256,256]{2,1,0:T(8,128)}, f32[2,256,256]{2,1,0:T(8,128)}, f32[2,256,256]{2,1,0:T(8,128)}), (f32[2,256,256]{2,1,0:T(8,128)}, f32[2,256,256]{2,1,0:T(8,128)}, f32[2,256,256]{2,1,0:T(8,128)})) %all-reduce.5.cloned.1.call-update) | async-done | bytes 1572880 | tf_op jit(solution)/shard_map/psum | solution.py:98
  222.7 1.7 fusion.54
  231.9 2.0 fusion.53
  238.3 9.0 %all-to-all-start.4 = ((bf16[8,128,512]{1,2,0:T(8,128)(2,1)}), bf16[8,128,512]{1,2,0:T(8,128)(2,1)}, u32[]{:S(2)}, u32[]{:S(2)}) async-start(bf16[8,128,512]{1,2,0:T(8,128)(2,1)} %copy.139), calls=%async_computation.4 | async-start | bytes 2097152 | tf_op jit(solution)/shard_map/all_to_all | solution.py:120
  247.3 130.5 %all-reduce.7.cloned.1.call-done = (bf16[2,256,256]{2,1,0:T(8,128)(2,1)}, bf16[2,256,256]{2,1,0:T(8,128)(2,1)}, bf16[2,256,256]{2,1,0:T(8,128)(2,1)}) async-done(((bf16[2,256,256]{2,1,0:T(8,128)(2,1)}, bf16[2,256,256]{2,1,0:T(8,128)(2,1)}, bf16[2,256,256]{2,1,0:T(8,128)(2,1)}), (bf16[2,256,256]{2,1,0:T(8,128)(2,1)}, bf16[2,256,256]{2,1,0:T(8,128)(2,1)}, ...) | async-done | bytes 786448 | tf_op jit(solution)/shard_map/psum | solution.py:108
  377.8 2.9 fusion.41
  383.4 2.1 copy-done.1
  385.5 2.3 fusion.6
  387.8 1.8 fusion.39
  393.7 6.0 %fusion.32 = f32[2,1024,256]{2,1,0:T(8,128)} fusion(bf16[2,256,256]{2,1,0:T(8,128)(2,1)} %param.13, f32[2,1024,256]{2,1,0:T(8,128)S(1)} %copy-done.3, f32[2,256,1024]{1,2,0:T(8,128)} %copy-done.17, f32[2,1024,256]{2,1,0:T(8,128)S(1)} %copy-done.5, f32[2,1024,256]{2,1,0:T(8,128)} %get-tuple-element.20, f32[2,1024,256]{2,1,0:T(8,128)S(1)} %copy-done.1, ...), kind=kOutput, calls=%fused_computation.57 | convolution fusion | flops 279969792 | bytes 14942208 | tf_op jit(solution)/shard_map/vmap()/dot_general | solution.py:70
  399.7 9.7 %all-to-all-start.6 = ((bf16[8,128,512]{1,2,0:T(8,128)(2,1)}), bf16[8,128,512]{1,2,0:T(8,128)(2,1)}, u32[]{:S(2)}, u32[]{:S(2)}) async-start(bf16[8,128,512]{1,2,0:T(8,128)(2,1)} %copy.155), calls=%async_computation.6 | async-start | bytes 2097152 | tf_op jit(solution)/shard_map/all_to_all | solution.py:122
  411.0 5.9 %fusion.22 = bf16[1024,2,256]{2,0,1:T(8,128)(2,1)} fusion(bf16[2,256,256]{2,1,0:T(8,128)(2,1)S(1)} %copy-done.13, f32[2,1024,256]{2,1,0:T(8,128)} %fusion.32, f32[2,1024,256]{2,1,0:T(8,128)S(1)} %fusion.37, f32[2,1024,256]{2,1,0:T(8,128)} %fusion.39, f32[2,1024,256]{2,1,0:T(8,128)} %fusion.41, f32[2,1024,256]{2,1,0:T(8,128)S(1)} %copy-done.4, ...), kind=kOutput, calls=%fused_computation.44 | convolution fusion | flops 277348352 | bytes 15990784 | tf_op jit(solution)/shard_map/vmap()/dot_general | solution.py:71
  419.8 4.8 %all-to-all-done.6 = bf16[8,128,512]{1,2,0:T(8,128)(2,1)} async-done(((bf16[8,128,512]{1,2,0:T(8,128)(2,1)}), bf16[8,128,512]{1,2,0:T(8,128)(2,1)}, u32[]{:S(2)}, u32[]{:S(2)}) %all-to-all-start.6) | async-done | bytes 1048608 | tf_op jit(solution)/shard_map/all_to_all | solution.py:122
  424.6 4.3 all-to-all-start.5
  428.9 2.3 copy.156
  431.2 2.3 copy.158
  433.4 10.6 %all-to-all-done.5 = bf16[8,128,512]{1,2,0:T(8,128)(2,1)S(1)} async-done(((bf16[8,128,512]{1,2,0:T(8,128)(2,1)}), bf16[8,128,512]{1,2,0:T(8,128)(2,1)S(1)}, u32[]{:S(2)}, u32[]{:S(2)}) %all-to-all-start.5) | async-done | bytes 1048608 | tf_op jit(solution)/shard_map/all_to_all | solution.py:121
  (106 shorter events, 38.5 us)
Async XLA Ops:
  7.2 9.1 %copy-start.20 = (bf16[128,4096]{1,0:T(8,128)(2,1)S(1)}, bf16[128,4096]{1,0:T(8,128)(2,1)}, u32[]{:S(2)}) copy-start(bf16[128,4096]{1,0:T(8,128)(2,1)} %param.10) | copy-start | bytes 3145732
  9.5 21.8 %all-to-all-start = ((bf16[128,8,512]{0,2,1:T(8,128)(2,1)}), bf16[128,8,512]{0,2,1:T(8,128)(2,1)S(1)}, u32[]{:S(2)}, u32[]{:S(2)}) async-start(bf16[128,8,512]{0,2,1:T(8,128)(2,1)} %bitcast), calls=%async_computation | async-start | bytes 2097152 | tf_op jit(solution)/shard_map/all_to_all | solution.py:81
  16.2 19.5 %copy-start.21 = (bf16[128,4096]{1,0:T(8,128)(2,1)S(1)}, bf16[128,4096]{1,0:T(8,128)(2,1)}, u32[]{:S(2)}) copy-start(bf16[128,4096]{1,0:T(8,128)(2,1)} %param.8) | copy-start | bytes 3145732
  31.3 19.5 %all-to-all-start.1 = ((bf16[128,8,512]{0,2,1:T(8,128)(2,1)}), bf16[128,8,512]{0,2,1:T(8,128)(2,1)S(1)}, u32[]{:S(2)}, u32[]{:S(2)}) async-start(bf16[128,8,512]{0,2,1:T(8,128)(2,1)} %bitcast.2), calls=%async_computation.1 | async-start | bytes 2097152 | tf_op jit(solution)/shard_map/all_to_all | solution.py:82
  50.8 23.2 %all-to-all-start.3 = ((bf16[128,8,512]{0,2,1:T(8,128)(2,1)}), bf16[128,8,512]{0,2,1:T(8,128)(2,1)}, u32[]{:S(2)}, u32[]{:S(2)}) async-start(bf16[128,8,512]{0,2,1:T(8,128)(2,1)} %bitcast.9), calls=%async_computation.3 | async-start | bytes 2097152 | tf_op jit(solution)/shard_map/all_to_all | solution.py:80
  55.8 166.9 %all-reduce.5.cloned.1.call-start = ((), (), s32[]{:S(2)}) async-start(), calls=%async_computation.7 | async-start | bytes 3145728 | tf_op jit(solution)/shard_map/psum | solution.py:98
  58.7 2.9 copy-start.31
  61.6 2.0 copy-start.14
  64.6 3.8 copy-start
  65.7 2.7 copy-start.2
  68.4 3.0 copy-start.7
  68.4 3.0 copy-start.11
  68.4 3.0 copy-start.9
  74.0 20.0 %all-to-all-start.2 = ((bf16[128,8,512]{0,2,1:T(8,128)(2,1)}), bf16[128,8,512]{0,2,1:T(8,128)(2,1)}, u32[]{:S(2)}, u32[]{:S(2)}) async-start(bf16[128,8,512]{0,2,1:T(8,128)(2,1)} %bitcast.4), calls=%async_computation.2 | async-start | bytes 2097152 | tf_op jit(solution)/shard_map/all_to_all | solution.py:83
  78.8 299.0 %all-reduce.7.cloned.1.call-start = ((), (), s32[]{:S(2)}) async-start(), calls=%async_computation.8 | async-start | bytes 1572864 | tf_op jit(solution)/shard_map/psum | solution.py:108
  228.5 2.1 copy-start.24
  231.8 2.0 copy-start.16
  231.9 2.0 copy-start.19
  238.3 161.4 %all-to-all-start.4 = ((bf16[8,128,512]{1,2,0:T(8,128)(2,1)}), bf16[8,128,512]{1,2,0:T(8,128)(2,1)}, u32[]{:S(2)}, u32[]{:S(2)}) async-start(bf16[8,128,512]{1,2,0:T(8,128)(2,1)} %copy.139), calls=%async_computation.4 | async-start | bytes 2097152 | tf_op jit(solution)/shard_map/all_to_all | solution.py:120
  247.3 133.4 %copy-start.12 = (bf16[2,1024,256]{2,1,0:T(8,128)(2,1)S(1)}, bf16[2,1024,256]{2,1,0:T(8,128)(2,1)}, u32[]{:S(2)}) copy-start(bf16[2,1024,256]{2,1,0:T(8,128)(2,1)} %copy-done.11) | copy-start | bytes 3145732
  377.8 2.9 copy-start.27
  381.7 1.8 copy-start.33
  382.2 5.6 %copy-start.6 = (f32[2,256,1024]{1,2,0:T(8,128)}, f32[2,256,1024]{1,2,0:T(8,128)S(1)}, u32[]{:S(2)}) copy-start(f32[2,256,1024]{1,2,0:T(8,128)S(1)} %fusion.36) | copy-start | bytes 6291460
  382.2 3.3 copy-start.1
  382.3 3.3 copy-start.30
  382.8 5.0 %copy-start.17 = (f32[2,256,1024]{1,2,0:T(8,128)}, f32[2,256,1024]{1,2,0:T(8,128)S(1)}, u32[]{:S(2)}) copy-start(f32[2,256,1024]{1,2,0:T(8,128)S(1)} %fusion.38) | copy-start | bytes 6291460
  385.5 2.3 copy-start.10
  391.1 1.9 copy-start.3
  391.2 2.6 copy-start.5
  399.7 9.7 %copy-start.8 = (bf16[2,1024,256]{2,1,0:T(8,128)(2,1)S(1)}, bf16[2,1024,256]{2,1,0:T(8,128)(2,1)}, u32[]{:S(2)}) copy-start(bf16[2,1024,256]{2,1,0:T(8,128)(2,1)} %copy-done.7) | copy-start | bytes 3145732
  399.7 24.9 %all-to-all-start.6 = ((bf16[8,128,512]{1,2,0:T(8,128)(2,1)}), bf16[8,128,512]{1,2,0:T(8,128)(2,1)}, u32[]{:S(2)}, u32[]{:S(2)}) async-start(bf16[8,128,512]{1,2,0:T(8,128)(2,1)} %copy.155), calls=%async_computation.6 | async-start | bytes 2097152 | tf_op jit(solution)/shard_map/all_to_all | solution.py:122
  424.6 19.5 %all-to-all-start.5 = ((bf16[8,128,512]{1,2,0:T(8,128)(2,1)}), bf16[8,128,512]{1,2,0:T(8,128)(2,1)S(1)}, u32[]{:S(2)}, u32[]{:S(2)}) async-start(bf16[8,128,512]{1,2,0:T(8,128)(2,1)} %copy.153), calls=%async_computation.5 | async-start | bytes 2097152 | tf_op jit(solution)/shard_map/all_to_all | solution.py:121
  (11 other events, 14.2 us)
Sparse Core Ops, SparseCore 0:
  72.8 149.8 all-reduce.4
  232.0 145.8 all-reduce.6
where the time goes:
time: 453 us; the launch traced here: 452 us
  waiting for transfers between devices  307 us (68%)
  local copies, waits for them, and re-layouts  45.4 us (10%)
  starting transfers between devices  43.8 us (10%)
  matrix products  39.9 us (9%)
  between operations  14.4 us (3%)
    psum x1, waiting for transfers between devices, body(): lax.psum(sums[1].astype(jnp.bfloat16), 'tok').astype(jnp.float32)  131 us
    psum x1, waiting for transfers between devices, body(): lax.psum((delta_gate, delta_up, delta_down), 'tok')  123 us
    unnamed x78, local copies, waits for them, and re-layouts  21.2 us
    all_to_all x1, waiting for transfers between devices, body(): lax.all_to_all(key_tokens, 'head', split_axis=1, concat_axis=0, tiled=True)  13.8 us
    all_to_all x1, waiting for transfers between devices, body(): lax.all_to_all(values, 'head', split_axis=1, concat_axis=0, tiled=True)  12.6 us
    all_to_all x1, waiting for transfers between devices, body(): lax.all_to_all(out_grad, 'head', split_axis=1, concat_axis=0, tiled=True)  10.8 us
    all_to_all x1, waiting for transfers between devices, body(): lax.all_to_all(key_flat, 'head', split_axis=0, concat_axis=1, tiled=True)  10.6 us
    all_to_all x1, starting transfers between devices, body(): lax.all_to_all(value_flat, 'head', split_axis=0, concat_axis=1, tiled=True)  9.66 us
  transfers between devices with their start and end apart: 9, of which 7 were waited for; matrix products, arithmetic and copies ran while one was open for 15% of the time, Pallas kernels for 0%

commit v1 on v0

v1 whole, which is shorter than its diff:
```python
import functools
import math

import jax
import jax.numpy as jnp
from jax import lax
from jax.experimental import pallas as pl
from jax.experimental.pallas import tpu as pltpu
from jax.sharding import PartitionSpec as P

DH = 256
NX, NZ, NY, NC = 4, 8, 4, 2
NH = NY * NC
ROWS = 128
ALL = NH * ROWS
PART = 3 * DH // NX
CHUNK = 256
MESH = pl.DeviceIdType.MESH
F32 = jnp.float32
BF16 = jnp.bfloat16


def mm(a, b):
    return jnp.dot(a, b, preferred_element_type=F32)


def mm_rt(a, b):
    return lax.dot_general(a, b, (((1,), (1,)), ((), ())), preferred_element_type=F32)


def mm_lt(a, b):
    return lax.dot_general(a, b, (((0,), (0,)), ((), ())), preferred_element_type=F32)


def kernel(
    scale,
    q_in, k_in, v_in, o_in, lr_in, wg_in, wu_in, wd_in,
    gq_out, gk_out, gv_out,
    buf, lr, w, acc, pb, rx, zf, zs, rz, full,
    gate, upper, dhid, hid, dgate, dup, scaled, stage,
    in_send, in_recv, in_loc, w_sem, lr_sem,
    xs, xr, zsd, zrv, azs, azr, axs, axr,
    out_send, out_recv, out_loc,
):
    tok, me = lax.axis_index("tok"), lax.axis_index("head")
    x, z = tok // NZ, tok % NZ
    y, c = me // NC, me % NC
    ins = (k_in, v_in, q_in, o_in)
    outs = (gq_out, gk_out, gv_out)

    ypeers = [(2, 0), (2, 1), (1, 0), (3, 0), (1, 1), (3, 1), (0, 1)]
    hpeers = [lax.rem(y + dy, NY) * NC + lax.rem(c + dc, NC) for dy, dc in ypeers]
    xpeers = [lax.rem(x + d, NX) for d in (2, 1, 3)]
    zds = (4, 3, 5, 2, 6, 1, 7)
    zpeers = [lax.rem(z + d, NZ) for d in zds]

    def xdev(px):
        return (px * NZ + z, me)

    def zdev(pz):
        return (x * NZ + pz, me)

    barrier = pltpu.get_barrier_semaphore()
    for p in hpeers:
        pl.semaphore_signal(barrier, inc=1, device_id=(tok, p), device_id_type=MESH)
    for p in xpeers:
        pl.semaphore_signal(barrier, inc=1, device_id=xdev(p), device_id_type=MESH)
    for p in zpeers:
        pl.semaphore_signal(barrier, inc=1, device_id=zdev(p), device_id_type=MESH)

    loc = []

    def cols(p, h):
        return pl.ds(pl.multiple_of(p * (2 * DH) + h * DH, DH), DH)

    def rows_of(p):
        return pl.ds(pl.multiple_of(p * ROWS, ROWS), ROWS)

    def local_in(a, h):
        cp = pltpu.make_async_copy(ins[a].at[:, cols(me, h)], buf.at[a, h, rows_of(me)], in_loc.at[a, h])
        cp.start()
        return cp

    wcp = []
    for h in range(2):
        for m, ref in enumerate((wg_in, wu_in, wd_in)):
            cp = pltpu.make_async_copy(ref.at[h], w.at[h, pl.ds(m * DH, DH)], w_sem.at[h, m])
            cp.start()
            wcp.append(cp)
    lcp = pltpu.make_async_copy(lr_in, lr, lr_sem)
    lcp.start()
    locals_in = {(a, h): local_in(a, h) for h in range(2) for a in range(4)}

    pl.semaphore_wait(barrier, len(hpeers) + len(xpeers) + len(zpeers))

    def send_in(a, h):
        for p in hpeers:
            pltpu.make_async_remote_copy(
                src_ref=ins[a].at[:, cols(p, h)],
                dst_ref=buf.at[a, h, rows_of(me)],
                send_sem=in_send.at[a, h],
                recv_sem=in_recv.at[a, h],
                device_id=(tok, p),
                device_id_type=MESH,
            ).start()

    def wait_bytes(ref, sem):
        pltpu.make_async_copy(ref, ref, sem).wait()

    def wait_in(a, h):
        locals_in[(a, h)].wait()
        wait_bytes(buf.at[a, h, pl.ds(0, ALL - ROWS)], in_recv.at[a, h])

    def key_forward(h):
        acc[0, h] = jnp.zeros((3 * DH, DH), F32)

        def step(j, carry):
            rows = pl.ds(pl.multiple_of(j * CHUNK, CHUNK), CHUNK)
            kr = buf[0, h, rows]
            sc = (lr[rows, h:h + 1] * buf[1, h, rows].astype(F32)).astype(BF16)
            scaled[h, rows] = sc
            gp = mm(kr, w[h, 0:DH])
            up = mm(kr, w[h, DH:2 * DH])
            kd = mm_rt(sc, w[h, 2 * DH:3 * DH])
            s = jax.nn.sigmoid(gp)
            act = gp * s
            slope = s * (1.0 + gp * (1.0 - s))
            hd = (act * up).astype(BF16)
            dg = (kd * up * slope).astype(BF16)
            du = (kd * act).astype(BF16)
            gate[h, rows] = gp
            upper[h, rows] = up
            dhid[h, rows] = kd
            hid[h, rows] = hd
            dgate[h, rows] = dg
            dup[h, rows] = du
            acc[0, h, 0:DH] += mm_lt(kr, dg)
            acc[0, h, DH:2 * DH] += mm_lt(kr, du)
            acc[0, h, 2 * DH:3 * DH] += mm_lt(hd, sc)
            return carry

        lax.fori_loop(0, ALL // CHUNK, step, 0)

    def part(p):
        return pl.ds(pl.multiple_of(p * PART, 16), PART)

    def rs_x_start(f, h):
        pb[f, h] = acc[f, h].astype(BF16)
        for i, p in enumerate(xpeers):
            pltpu.make_async_remote_copy(
                src_ref=pb.at[f, h, part(p)],
                dst_ref=rx.at[f, h, i],
                send_sem=xs.at[f, h],
                recv_sem=xr.at[f, h],
                device_id=xdev(p),
                device_id_type=MESH,
            ).start()

    def prow(p):
        return pl.multiple_of((p // 2) * 48, 16)

    def pcol(p):
        return pl.ds(pl.multiple_of((p % 2) * 128, 128), 128)

    def rs_x_finish(f, h):
        wait_bytes(rx.at[f, h], xr.at[f, h])
        total = acc[f, h, part(x)]
        for i in range(3):
            total = total + rx[f, h, i].astype(F32)
        zf[f, h] = total
        zs[f, h] = total.astype(BF16)
        for i, p in enumerate(zpeers):
            pltpu.make_async_remote_copy(
                src_ref=zs.at[f, h, pl.ds(prow(p), 48), pcol(p)],
                dst_ref=rz.at[f, h, i],
                send_sem=zsd.at[f, h],
                recv_sem=zrv.at[f, h],
                device_id=zdev(p),
                device_id_type=MESH,
            ).start()

    def rs_z_finish(f, h):
        wait_bytes(rz.at[f, h], zrv.at[f, h])
        total = zf[f, h, pl.ds(prow(z), 48), pcol(z)]
        for i in range(7):
            total = total + rz[f, h, i].astype(F32)
        own = pl.ds(pl.multiple_of(x * PART + prow(z), 16), 48)
        total = total * scale
        if f == 0:
            total = w[h, own, pcol(z)].astype(F32) + total
        full[f, h, own, pcol(z)] = total.astype(BF16)
        for p in zpeers:
            pltpu.make_async_remote_copy(
                src_ref=full.at[f, h, own, pcol(z)],
                dst_ref=full.at[f, h, own, pcol(z)],
                send_sem=azs.at[f, h],
                recv_sem=azr.at[f, h],
                device_id=zdev(p),
                device_id_type=MESH,
            ).start()

    def ag_z_finish(f, h):
        wait_bytes(rz.at[f, h], azr.at[f, h])
        for p in xpeers:
            pltpu.make_async_remote_copy(
                src_ref=full.at[f, h, part(x)],
                dst_ref=full.at[f, h, part(x)],
                send_sem=axs.at[f, h],
                recv_sem=axr.at[f, h],
                device_id=xdev(p),
                device_id_type=MESH,
            ).start()

    def ag_x_finish(f, h):
        wait_bytes(rx.at[f, h], axr.at[f, h])

    def send_out(a, h, yy, own_chip):
        def remote(p):
            pltpu.make_async_remote_copy(
                src_ref=stage.at[a, h, rows_of(p)],
                dst_ref=outs[a].at[:, cols(me, h)],
                send_sem=out_send.at[a, h],
                recv_sem=out_recv.at[a, h],
                device_id=(tok, p),
                device_id_type=MESH,
            ).start()

        @pl.when(jnp.logical_not(own_chip))
        def _():
            for cc in range(NC):
                remote(yy * NC + cc)

        @pl.when(own_chip)
        def _():
            remote(y * NC + (1 - c))
            pltpu.make_async_copy(
                stage.at[a, h, rows_of(me)], outs[a].at[:, cols(me, h)], out_loc.at[a, h]
            ).start()

    def query_side(h):
        acc[1, h] = jnp.zeros((3 * DH, DH), F32)

        def step(j, carry):
            yy = lax.rem(y + 1 + j, NY)
            rows = pl.ds(pl.multiple_of(yy * CHUNK, CHUNK), CHUNK)
            qr = buf[2, h, rows]
            orr = buf[3, h, rows]
            ng = full[0, h, 0:DH]
            nu = full[0, h, DH:2 * DH]
            gp = mm(qr, ng)
            up = mm(qr, nu)
            qd = mm_rt(orr, full[0, h, 2 * DH:3 * DH])
            s = jax.nn.sigmoid(gp)
            act = gp * s
            slope = s * (1.0 + gp * (1.0 - s))
            hd = (act * up).astype(BF16)
            dg = (qd * up * slope).astype(BF16)
            du = (qd * act).astype(BF16)
            stage[0, h, rows] = (mm_rt(dg, ng) + mm_rt(du, nu)).astype(BF16)
            send_out(0, h, yy, j == NY - 1)
            acc[1, h, 0:DH] += mm_lt(qr, dg)
            acc[1, h, DH:2 * DH] += mm_lt(qr, du)
            acc[1, h, 2 * DH:3 * DH] += mm_lt(hd, orr)
            return carry

        lax.fori_loop(0, NY, step, 0)

    def key_back(h):
        def step(j, carry):
            yy = lax.rem(y + 1 + j, NY)
            rows = pl.ds(pl.multiple_of(yy * CHUNK, CHUNK), CHUNK)
            kr = buf[0, h, rows]
            ag = full[1, h, 0:DH]
            au = full[1, h, DH:2 * DH]
            ad = full[1, h, 2 * DH:3 * DH]
            bdg = mm(kr, ag)
            bdu = mm(kr, au)
            bh = mm_rt(scaled[h, rows], ad)
            gp = gate[h, rows]
            up = upper[h, rows]
            kd = dhid[h, rows]
            s = jax.nn.sigmoid(gp)
            act = gp * s
            slope = s * (1.0 + gp * (1.0 - s))
            curve = s * (1.0 - s) * (2.0 + gp * (1.0 - 2.0 * s))
            bdh = (bdg * up * slope + bdu * act).astype(BF16)
            bg = (bdg * kd * up * curve + (bdu * kd + bh * up) * slope).astype(BF16)
            bu = (bdg * kd * slope + bh * act).astype(BF16)
            kg = mm_rt(dgate[h, rows], ag) + mm_rt(dup[h, rows], au)
            kg = kg + mm_rt(bg, w[h, 0:DH]) + mm_rt(bu, w[h, DH:2 * DH])
            stage[1, h, rows] = kg.astype(BF16)
            send_out(1, h, yy, j == NY - 1)
            vg = mm(hid[h, rows], ad) + mm(bdh, w[h, 2 * DH:3 * DH])
            stage[2, h, rows] = (lr[rows, h:h + 1] * vg).astype(BF16)
            send_out(2, h, yy, j == NY - 1)
            return carry

        lax.fori_loop(0, NY, step, 0)

    for h in range(2):
        send_in(0, h)
        send_in(1, h)
    for cp in wcp:
        cp.wait()
    lcp.wait()

    wait_in(0, 0)
    wait_in(1, 0)
    send_in(2, 0)
    send_in(3, 0)
    key_forward(0)
    rs_x_start(0, 0)
    rs_x_finish(0, 0)
    wait_in(0, 1)
    wait_in(1, 1)
    send_in(2, 1)
    send_in(3, 1)
    key_forward(1)
    rs_x_start(0, 1)
    rs_z_finish(0, 0)
    ag_z_finish(0, 0)
    rs_x_finish(0, 1)
    rs_z_finish(0, 1)
    ag_z_finish(0, 1)
    ag_x_finish(0, 0)
    wait_in(2, 0)
    wait_in(3, 0)
    query_side(0)
    rs_x_start(1, 0)
    ag_x_finish(0, 1)
    rs_x_finish(1, 0)
    wait_in(2, 1)
    wait_in(3, 1)
    query_side(1)
    rs_x_start(1, 1)
    rs_z_finish(1, 0)
    ag_z_finish(1, 0)
    rs_x_finish(1, 1)
    rs_z_finish(1, 1)
    ag_x_finish(1, 0)
    key_back(0)
    ag_z_finish(1, 1)
    ag_x_finish(1, 1)
    key_back(1)

    for h in range(2):
        for a in range(4):
            wait_bytes(buf.at[a, h, pl.ds(0, ALL - ROWS)], in_send.at[a, h])
        for f in range(2):
            wait_bytes(rx.at[f, h], xs.at[f, h])
            wait_bytes(rz.at[f, h], zsd.at[f, h])
            wait_bytes(rz.at[f, h], azs.at[f, h])
            wait_bytes(rx.at[f, h], axs.at[f, h])
        for a in range(3):
            wait_bytes(stage.at[a, h, pl.ds(0, ALL - ROWS)], out_send.at[a, h])
            wait_bytes(stage.at[a, h, pl.ds(0, ALL - ROWS)], out_recv.at[a, h])
            wait_bytes(stage.at[a, h, pl.ds(0, ROWS)], out_loc.at[a, h])


def body(queries, key_tokens, values, out_grad, learn_rates, w_gate, w_up, w_down):
    scale = 1.0 / math.sqrt(DH * ALL * NX * NZ)
    dma = pltpu.SemaphoreType.DMA
    out = jax.ShapeDtypeStruct(queries.shape, BF16)
    return pl.pallas_call(
        functools.partial(kernel, scale),
        out_shape=(out, out, out),
        in_specs=[pl.BlockSpec(memory_space=pl.ANY)] * 8,
        out_specs=[pl.BlockSpec(memory_space=pl.ANY)] * 3,
        scratch_shapes=[
            pltpu.VMEM((4, 2, ALL, DH), BF16),
            pltpu.VMEM((ALL, 2), F32),
            pltpu.VMEM((2, 3 * DH, DH), BF16),
            pltpu.VMEM((2, 2, 3 * DH, DH), F32),
            pltpu.VMEM((2, 2, 3 * DH, DH), BF16),
            pltpu.VMEM((2, 2, NX - 1, PART, DH), BF16),
            pltpu.VMEM((2, 2, PART, DH), F32),
            pltpu.VMEM((2, 2, PART, DH), BF16),
            pltpu.VMEM((2, 2, NZ - 1, 48, 128), BF16),
            pltpu.VMEM((2, 2, 3 * DH, DH), BF16),
            pltpu.VMEM((2, ALL, DH), F32),
            pltpu.VMEM((2, ALL, DH), F32),
            pltpu.VMEM((2, ALL, DH), F32),
            pltpu.VMEM((2, ALL, DH), BF16),
            pltpu.VMEM((2, ALL, DH), BF16),
            pltpu.VMEM((2, ALL, DH), BF16),
            pltpu.VMEM((2, ALL, DH), BF16),
            pltpu.VMEM((3, 2, ALL, DH), BF16),
            dma((4, 2)), dma((4, 2)), dma((4, 2)), dma((2, 3)), dma,
            dma((2, 2)), dma((2, 2)), dma((2, 2)), dma((2, 2)),
            dma((2, 2)), dma((2, 2)), dma((2, 2)), dma((2, 2)),
            dma((3, 2)), dma((3, 2)), dma((3, 2)),
        ],
        compiler_params=pltpu.CompilerParams(
            collective_id=0, has_side_effects=True, vmem_limit_bytes=48 << 20
        ),
    )(queries, key_tokens, values, out_grad, learn_rates, w_gate, w_up, w_down)


def solution(mesh):
    tokens = P(("tok", "head"), None)
    heads = P("head", None, None)
    return jax.shard_map(
        body,
        mesh=mesh,
        in_specs=(tokens, tokens, tokens, tokens, P("tok", "head"), heads, heads, heads),
        out_specs=(tokens, tokens, tokens),
        check_vma=False,
    )
```

time: 453 us -> 111 us (0.25)
  waiting for transfers between devices: 307 us -> 0 us
  Pallas kernels: 0 us -> 103 us
  starting transfers between devices: 43.8 us -> 0 us
  matrix products: 39.9 us -> 0 us
  local copies, waits for them, and re-layouts: 45.4 us -> 6.1 us
  between operations: 14.4 us -> 0.67 us
    psum x2 -> x0, waiting for transfers between devices: 254 us -> none  [the longest x1 131 us: body(): lax.psum(sums[1].astype(jnp.bfloat16), 'tok').astype(jnp.float32)]
    pallas_call x0 -> x1, Pallas kernels: none -> 103 us  [body(): pl.pallas_call(functools.partial(kernel, scale), out_shape=(out, out, out...]
    all_to_all x7 -> x0, waiting for transfers between devices: 52.6 us -> none  [the longest x1 13.8 us: body(): lax.all_to_all(key_tokens, 'head', split_axis=1, concat_axis=0, tiled=True)]
    all_to_all x7 -> x0, starting transfers between devices: 43.8 us -> none  [the longest x1 9.66 us: body(): lax.all_to_all(value_flat, 'head', split_axis=0, concat_axis=1, tiled=True)]
    dot_general x23 -> x0, matrix products: 39.9 us -> none  [the longest x1 5.96 us: key_back(): jnp.dot(back_gate, gate_mat.T, preferred_element_type=jnp.float32)]
    unnamed x78 -> x12, local copies, waits for them, and re-layouts: 21.2 us -> 6.1 us
    convert_element_type x6 -> x0, local copies, waits for them, and re-layouts: 9.95 us -> none  [the longest x3 5.68 us: body(): by_head(value_all).astype(jnp.float32)]
    all_to_all x6 -> x0, local copies, waits for them, and re-layouts: 9.88 us -> none  [the longest x1 2.88 us: body(): lax.all_to_all(out_grad, 'head', split_axis=1, concat_axis=0, tiled=True)]
  transfers between devices with their start and end apart: 9 -> 0, of which waited for: 7 -> 0; matrix products, arithmetic and copies ran while one was open for 15% -> 0% of each run, Pallas kernels for 0% -> 0%
where the time goes in v1:
time: 111 us; the launch traced here: 110 us
  Pallas kernels  103 us (93%)
  local copies, waits for them, and re-layouts  6.1 us (5%)
    pallas_call x1, Pallas kernels, body(): pl.pallas_call(functools.partial(kernel, scale), out_shape=(out, out, out...  103 us
    unnamed x12, local copies, waits for them, and re-layouts  6.1 us

profile of v1, /device:TPU:1, one launch (start us, length us, event | category | flops | bytes accessed | tf_op | source)
XLA Modules:
  0.0 110.0 jit_solution(10077927981954951142)
XLA Ops:
  0.6 0.0 copy-start.2
  0.6 0.0 copy-start.1
  0.7 1.0 copy.11.lr_in
  1.6 0.0 copy-done.2
  1.6 0.0 copy-done.1
  1.7 0.0 copy-start
  1.7 1.2 %copy-done = bf16[128,4096]{1,0:T(8,128)(2,1)S(1)} copy-done((bf16[128,4096]{1,0:T(8,128)(2,1)S(1)}, bf16[128,4096]{1,0:T(8,128)(2,1)}, u32[]{:S(2)}) %copy-start) | copy-done | bytes 1048600
  2.9 0.0 copy-start.3
  2.9 0.9 copy-done.3
  3.9 103.2 %shard_map.103 = (bf16[128,4096]{1,0:T(8,128)(2,1)S(1)}, bf16[128,4096]{1,0:T(8,128)(2,1)S(1)}, bf16[128,4096]{1,0:T(8,128)(2,1)S(1)}) custom-call(bf16[128,4096]{1,0:T(8,128)(2,1)S(1)} %copy-done, bf16[128,4096]{1,0:T(8,128)(2,1)} %k_in.1, bf16[128,4096]{1,0:T(8,128)(2,1)} %v_in.1, bf16[128,4096]{1,0:T(8,128)(2,1)} %o_in.1, f32[1024,2]{1,0:T(8,128)S(1)} %copy.11.lr_in, ...), custom_call_target="tpu_custom_call" | custom-call | tf_op jit(solution)/shard_map/pallas_call | solution.py:364
  107.1 1.0 copy.15
  108.1 1.0 copy.16
  109.0 1.0 copy.17
Async XLA Ops:
  0.6 1.0 copy-start.2
  0.6 1.0 copy-start.1
  1.7 1.2 %copy-start = (bf16[128,4096]{1,0:T(8,128)(2,1)S(1)}, bf16[128,4096]{1,0:T(8,128)(2,1)}, u32[]{:S(2)}) copy-start(bf16[128,4096]{1,0:T(8,128)(2,1)} %q_in.1) | copy-start | bytes 3145732
  2.9 0.9 copy-start.3

commit v2 on v1

v2 whole, which is shorter than its diff:
```python
import functools
import math

import jax
import jax.numpy as jnp
from jax import lax
from jax.experimental import pallas as pl
from jax.experimental.pallas import tpu as pltpu
from jax.sharding import PartitionSpec as P

DH = 256
NX, NZ, NY, NC = 4, 8, 4, 2
NH = NY * NC
ROWS = 128
ALL = NH * ROWS
PART = DH // NX
ZROWS, ZCOLS = 16, 128
EIGHTH = DH // NZ
CHUNK = 256
MESH = pl.DeviceIdType.MESH
F32 = jnp.float32
BF16 = jnp.bfloat16


def mm(a, b):
    return jnp.dot(a, b, preferred_element_type=F32)


def mm_rt(a, b):
    return lax.dot_general(a, b, (((1,), (1,)), ((), ())), preferred_element_type=F32)


def mm_lt(a, b):
    return lax.dot_general(a, b, (((0,), (0,)), ((), ())), preferred_element_type=F32)


def kernel(
    scale,
    q_in, k_in, v_in, o_in, lr_in, wg_in, wu_in, wd_in,
    gq_out, gk_out, gv_out,
    buf, lrc, lrow, lsend, lq, lfin, wz, w, acc, pb, rx, zf, zs, rz, full,
    gate, upper, dhid, hid, dgate, dup, scaled, stage,
    in_send, in_recv, in_loc, w_sem, lr_sem, w1s, w1r, w2s, w2r, l1s, l1r, l2s, l2r,
    xs, xr, zsd, zrv, azs, azr, axs, axr,
    out_send, out_recv, out_loc,
):
    tok, me = lax.axis_index("tok"), lax.axis_index("head")
    x, z = tok // NZ, tok % NZ
    y, c = me // NC, me % NC
    ins = (k_in, v_in, q_in, o_in)
    outs = (gq_out, gk_out, gv_out)

    spots = [(1, 0), (3, 0), (1, 1), (3, 1), (2, 0), (2, 1), (0, 1)]
    chip = (y, x)
    line = (me, x * NC + c)
    lpeers = [
        [(lax.rem(chip[g] + dp, NY) * NC + lax.rem(c + dc, NC)) for dp, dc in spots] for g in range(2)
    ]
    cpos = (x, y)
    cpeers = [[lax.rem(cpos[g] + d, NX) for d in (2, 1, 3)] for g in range(2)]
    zpeers = [lax.rem(z + d, NZ) for d in (4, 3, 5, 2, 6, 1, 7)]

    def ldev(g, p):
        return (tok, p) if g == 0 else ((p // NC) * NZ + z, y * NC + p % NC)

    def cdev(g, p):
        return (p * NZ + z, me) if g == 0 else (tok, p * NC + c)

    def zdev(pz):
        return (x * NZ + pz, me)

    barrier = pltpu.get_barrier_semaphore()
    greet = [ldev(0, p) for p in lpeers[0]] + [ldev(1, p) for p in lpeers[1][:-1]] + [zdev(p) for p in zpeers]
    for p in greet:
        pl.semaphore_signal(barrier, inc=1, device_id=p, device_id_type=MESH)

    def cols(p, h):
        return pl.ds(pl.multiple_of(p * (2 * DH) + h * DH, DH), DH)

    def rows_of(p):
        return pl.ds(pl.multiple_of(p * ROWS, ROWS), ROWS)

    def local_in(a, h):
        cp = pltpu.make_async_copy(ins[a].at[:, cols(line[h], h)], buf.at[a, h, rows_of(line[h])], in_loc.at[a, h])
        cp.start()
        return cp

    w_in = (wg_in, wu_in, wd_in)
    eighth = pl.ds(pl.multiple_of(z * EIGHTH, EIGHTH), EIGHTH)
    diagonal = x == y
    wcp = []
    for m in range(3):
        wcp.append(pltpu.make_async_copy(w_in[m].at[0], w.at[0, pl.ds(m * DH, DH)], w_sem.at[0, m]))
    lcp = pltpu.make_async_copy(lr_in, lrow, lr_sem)
    lcp.start()
    for cp in wcp:
        cp.start()
    locals_in = {(a, h): local_in(a, h) for h in range(2) for a in range(4)}
    lcp.wait()
    for i in range(NY):
        lsend[i] = jnp.broadcast_to(lrow[1:2, i * CHUNK:(i + 1) * CHUNK], (8, CHUNK))
    lq[y] = lsend[y]

    pl.semaphore_wait(barrier, len(greet))

    def column(row):
        return jnp.broadcast_to(row, (128, CHUNK)).T

    def weights_first():
        @pl.when(diagonal)
        def _():
            for m in range(3):
                pltpu.make_async_copy(w_in[m].at[1, eighth], wz.at[z, m], w_sem.at[1, m]).start()
                for p in cpeers[1]:
                    pltpu.make_async_remote_copy(
                        src_ref=w_in[m].at[1, eighth],
                        dst_ref=wz.at[z, m],
                        send_sem=w1s,
                        recv_sem=w1r,
                        device_id=cdev(1, p),
                        device_id_type=MESH,
                    ).start()

        for p in cpeers[1]:
            pltpu.make_async_remote_copy(
                src_ref=lsend.at[p],
                dst_ref=lq.at[y],
                send_sem=l1s,
                recv_sem=l1r,
                device_id=cdev(1, p),
                device_id_type=MESH,
            ).start()

    def weights_second():
        @pl.when(diagonal)
        def _():
            for m in range(3):
                wait_bytes(wz.at[0, m], w_sem.at[1, m])

        @pl.when(jnp.logical_not(diagonal))
        def _():
            wait_bytes(wz.at[0], w1r)

        for p in zpeers:
            pltpu.make_async_remote_copy(
                src_ref=wz.at[z],
                dst_ref=wz.at[z],
                send_sem=w2s,
                recv_sem=w2r,
                device_id=zdev(p),
                device_id_type=MESH,
            ).start()
        wait_bytes(lq.at[pl.ds(0, 3)], l1r)
        for p in cpeers[0]:
            pltpu.make_async_remote_copy(
                src_ref=lq.at[p],
                dst_ref=lfin.at[x],
                send_sem=l2s,
                recv_sem=l2r,
                device_id=cdev(0, p),
                device_id_type=MESH,
            ).start()
        lfin[x] = lq[x]
        for i in range(NY):
            lrc[0, pl.ds(i * CHUNK, CHUNK)] = column(lrow[0:1, i * CHUNK:(i + 1) * CHUNK])

    def weights_third():
        wait_bytes(wz.at[pl.ds(0, NZ - 1)], w2r)
        wait_bytes(lq.at[pl.ds(0, 3)], l2r)
        for i in range(NZ):
            for m in range(3):
                w[1, pl.ds(m * DH + i * EIGHTH, EIGHTH)] = wz[i, m]
        for i in range(NX):
            lrc[1, pl.ds(i * CHUNK, CHUNK)] = column(lfin[i, 0:1])

    def rates(h, rows):
        col = lrc[h, rows]
        return jnp.concatenate([col, col], axis=1)

    def send_in(a, h, which=range(7)):
        for p in [lpeers[h][i] for i in which]:
            pltpu.make_async_remote_copy(
                src_ref=ins[a].at[:, cols(p, h)],
                dst_ref=buf.at[a, h, rows_of(line[h])],
                send_sem=in_send.at[a, h],
                recv_sem=in_recv.at[a, h, chip[h]],
                device_id=ldev(h, p),
                device_id_type=MESH,
            ).start()

    def wait_bytes(ref, sem):
        pltpu.make_async_copy(ref, ref, sem).wait()

    def wait_in(a, h, off):
        cc = lax.rem(chip[h] + off, NY)
        if off == 0:
            locals_in[(a, h)].wait()
            wait_bytes(buf.at[a, h, pl.ds(0, ROWS)], in_recv.at[a, h, cc])
        else:
            wait_bytes(buf.at[a, h, pl.ds(0, CHUNK)], in_recv.at[a, h, cc])

    def silu_parts(gp):
        s = 0.5 * jnp.tanh(0.5 * gp) + 0.5
        act = gp * s
        rest = 1.0 - s
        return s, act, rest, s + act * rest

    def key_forward(h, off):
        wait_in(0, h, off)
        wait_in(1, h, off)
        cc = lax.rem(chip[h] + off, NY)
        rows = pl.ds(pl.multiple_of(cc * CHUNK, CHUNK), CHUNK)
        kr = buf[0, h, rows]
        sc = (rates(h, rows) * buf[1, h, rows].astype(F32)).astype(BF16)
        scaled[h, rows] = sc
        gp = mm(kr, w[h, 0:DH])
        up = mm(kr, w[h, DH:2 * DH])
        kd = mm_rt(sc, w[h, 2 * DH:3 * DH])
        s, act, rest, slope = silu_parts(gp)
        hd = (act * up).astype(BF16)
        dg = (kd * up * slope).astype(BF16)
        du = (kd * act).astype(BF16)
        gate[h, rows] = gp
        upper[h, rows] = up
        dhid[h, rows] = kd
        hid[h, rows] = hd
        dgate[h, rows] = dg
        dup[h, rows] = du
        for m, term in enumerate((mm_lt(kr, dg), mm_lt(kr, du), mm_lt(hd, sc))):
            mat = pl.ds(m * DH, DH)
            acc[0, h, mat] = term if off == 0 else acc[0, h, mat] + term

    def part(m, p):
        return pl.ds(pl.multiple_of(m * DH + p * PART, PART), PART)

    def zrow(p):
        return pl.multiple_of((p // 2) * ZROWS, ZROWS)

    def zcol(p):
        return pl.ds(pl.multiple_of((p % 2) * ZCOLS, ZCOLS), ZCOLS)

    def rs_x_start(f, h, m):
        mat = pl.ds(m * DH, DH)
        pb[f, h, mat] = acc[f, h, mat].astype(BF16)
        for i, p in enumerate(cpeers[h]):
            pltpu.make_async_remote_copy(
                src_ref=pb.at[f, h, part(m, p)],
                dst_ref=rx.at[f, h, m, i],
                send_sem=xs.at[f, h, m],
                recv_sem=xr.at[f, h, m],
                device_id=cdev(h, p),
                device_id_type=MESH,
            ).start()

    def rs_x_finish(f, h, m):
        wait_bytes(rx.at[f, h, m], xr.at[f, h, m])
        total = acc[f, h, part(m, cpos[h])]
        for i in range(NX - 1):
            total = total + rx[f, h, m, i].astype(F32)
        zf[f, h, m] = total
        zs[f, h, m] = total.astype(BF16)
        for i, p in enumerate(zpeers):
            pltpu.make_async_remote_copy(
                src_ref=zs.at[f, h, m, pl.ds(zrow(p), ZROWS), zcol(p)],
                dst_ref=rz.at[f, h, m, i],
                send_sem=zsd.at[f, h, m],
                recv_sem=zrv.at[f, h, m],
                device_id=zdev(p),
                device_id_type=MESH,
            ).start()

    def rs_z_finish(f, h, m):
        wait_bytes(rz.at[f, h, m], zrv.at[f, h, m])
        total = zf[f, h, m, pl.ds(zrow(z), ZROWS), zcol(z)]
        for i in range(NZ - 1):
            total = total + rz[f, h, m, i].astype(F32)
        own = pl.ds(pl.multiple_of(m * DH + cpos[h] * PART + zrow(z), ZROWS), ZROWS)
        total = total * scale
        if f == 0:
            total = w[h, own, zcol(z)].astype(F32) + total
        full[f, h, own, zcol(z)] = total.astype(BF16)
        for p in zpeers:
            pltpu.make_async_remote_copy(
                src_ref=full.at[f, h, own, zcol(z)],
                dst_ref=full.at[f, h, own, zcol(z)],
                send_sem=azs.at[f, h, m],
                recv_sem=azr.at[f, h, m],
                device_id=zdev(p),
                device_id_type=MESH,
            ).start()

    def ag_z_finish(f, h, m):
        wait_bytes(rz.at[f, h, m], azr.at[f, h, m])
        for p in cpeers[h]:
            pltpu.make_async_remote_copy(
                src_ref=full.at[f, h, part(m, cpos[h])],
                dst_ref=full.at[f, h, part(m, cpos[h])],
                send_sem=axs.at[f, h, m],
                recv_sem=axr.at[f, h, m],
                device_id=cdev(h, p),
                device_id_type=MESH,
            ).start()

    def ag_x_finish(f, h, m):
        wait_bytes(rx.at[f, h, m], axr.at[f, h, m])

    def send_out(a, h, cc, own_chip):
        def remote(p):
            pltpu.make_async_remote_copy(
                src_ref=stage.at[a, h, rows_of(p)],
                dst_ref=outs[a].at[:, cols(line[h], h)],
                send_sem=out_send.at[a, h],
                recv_sem=out_recv.at[a, h],
                device_id=ldev(h, p),
                device_id_type=MESH,
            ).start()

        @pl.when(jnp.logical_not(own_chip))
        def _():
            for core in range(NC):
                remote(cc * NC + core)

        @pl.when(own_chip)
        def _():
            remote(chip[h] * NC + (1 - c))
            pltpu.make_async_copy(
                stage.at[a, h, rows_of(line[h])], outs[a].at[:, cols(line[h], h)], out_loc.at[a, h]
            ).start()

    def chunk_of(h, j):
        cc = lax.rem(chip[h] + 2 + j + j // 2 + 2 * (j // 3), NY)
        return cc, pl.ds(pl.multiple_of(cc * CHUNK, CHUNK), CHUNK)

    def query_side(h):
        acc[1, h] = jnp.zeros((3 * DH, DH), F32)

        def step(j, carry):
            yy, rows = chunk_of(h, j)
            qr = buf[2, h, rows]
            orr = buf[3, h, rows]
            ng = full[0, h, 0:DH]
            nu = full[0, h, DH:2 * DH]
            gp = mm(qr, ng)
            up = mm(qr, nu)
            qd = mm_rt(orr, full[0, h, 2 * DH:3 * DH])
            s, act, rest, slope = silu_parts(gp)
            hd = (act * up).astype(BF16)
            dg = (qd * up * slope).astype(BF16)
            du = (qd * act).astype(BF16)
            stage[0, h, rows] = (mm_rt(dg, ng) + mm_rt(du, nu)).astype(BF16)
            acc[1, h, 0:DH] += mm_lt(qr, dg)
            acc[1, h, DH:2 * DH] += mm_lt(qr, du)
            acc[1, h, 2 * DH:3 * DH] += mm_lt(hd, orr)
            return carry

        lax.fori_loop(0, NY, step, 0)

    def back(h, j):
        yy, rows = chunk_of(h, j)
        kr = buf[0, h, rows]
        ag = full[1, h, 0:DH]
        au = full[1, h, DH:2 * DH]
        ad = full[1, h, 2 * DH:3 * DH]
        bdg = mm(kr, ag)
        bdu = mm(kr, au)
        bh = mm_rt(scaled[h, rows], ad)
        gp = gate[h, rows]
        up = upper[h, rows]
        kd = dhid[h, rows]
        s, act, rest, slope = silu_parts(gp)
        twice = s + s
        curve = rest * (twice + act * (1.0 - twice))
        bdh = (bdg * up * slope + bdu * act).astype(BF16)
        bg = (bdg * kd * up * curve + (bdu * kd + bh * up) * slope).astype(BF16)
        bu = (bdg * kd * slope + bh * act).astype(BF16)
        kg = mm_rt(dgate[h, rows], ag) + mm_rt(dup[h, rows], au)
        kg = kg + mm_rt(bg, w[h, 0:DH]) + mm_rt(bu, w[h, DH:2 * DH])
        stage[1, h, rows] = kg.astype(BF16)
        send_out(1, h, yy, j == NY - 1)
        vg = mm(hid[h, rows], ad) + mm(bdh, w[h, 2 * DH:3 * DH])
        stage[2, h, rows] = (rates(h, rows) * vg).astype(BF16)
        send_out(2, h, yy, j == NY - 1)

    def key_back():
        def step(j, carry):
            back(0, j)
            back(1, j)
            return carry

        lax.fori_loop(0, NY, step, 0)

    def send_query(h):
        for j in range(NY):
            cc, rows = chunk_of(h, j)
            if j < NY - 1:
                send_out(0, h, cc, False)
            else:
                send_out(0, h, cc, True)

    weights_first()
    for which in ((6,), (0, 1, 2, 3), (4, 5)):
        for a in (0, 1):
            for h in (0, 1):
                send_in(a, h, which)
    weights_second()
    for cp in wcp:
        cp.wait()
    for off in (0, 1, 3):
        key_forward(0, off)
    weights_third()
    for off in (0, 1, 3):
        key_forward(1, off)
    key_forward(0, 2)
    for m in range(3):
        rs_x_start(0, 0, m)
    send_in(2, 1)
    send_in(3, 1)
    key_forward(1, 2)
    for m in range(3):
        rs_x_start(0, 1, m)
    send_in(2, 0)
    send_in(3, 0)
    for step in (rs_x_finish, rs_z_finish, ag_z_finish):
        for h in range(2):
            for m in range(3):
                step(0, h, m)
    for h in range(2):
        for m in range(3):
            ag_x_finish(0, h, m)
        for off in range(NY):
            wait_in(2, h, off)
            wait_in(3, h, off)
        query_side(h)
        for m in range(3):
            rs_x_start(1, h, m)
    for h in range(2):
        send_query(h)
    for step in (rs_x_finish, rs_z_finish, ag_z_finish, ag_x_finish):
        for h in range(2):
            for m in range(3):
                step(1, h, m)
    key_back()

    @pl.when(diagonal)
    def _():
        wait_bytes(wz.at[pl.ds(0, 3)], w1s)

    wait_bytes(wz.at[pl.ds(0, NZ - 1)], w2s)
    wait_bytes(lq.at[pl.ds(0, 3)], l1s)
    wait_bytes(lq.at[pl.ds(0, 3)], l2s)
    for h in range(2):
        for a in range(4):
            wait_bytes(buf.at[a, h, pl.ds(0, ALL - ROWS)], in_send.at[a, h])
        for f in range(2):
            for m in range(3):
                wait_bytes(rx.at[f, h, m], xs.at[f, h, m])
                wait_bytes(rz.at[f, h, m], zsd.at[f, h, m])
                wait_bytes(rz.at[f, h, m], azs.at[f, h, m])
                wait_bytes(rx.at[f, h, m], axs.at[f, h, m])
        for a in range(3):
            wait_bytes(stage.at[a, h, pl.ds(0, ALL - ROWS)], out_send.at[a, h])
            wait_bytes(stage.at[a, h, pl.ds(0, ALL - ROWS)], out_recv.at[a, h])
            wait_bytes(stage.at[a, h, pl.ds(0, ROWS)], out_loc.at[a, h])


def body(queries, key_tokens, values, out_grad, learn_rates, w_gate, w_up, w_down):
    scale = 1.0 / math.sqrt(DH * ALL * NX * NZ)
    dma = pltpu.SemaphoreType.DMA
    out = jax.ShapeDtypeStruct(queries.shape, BF16)
    return pl.pallas_call(
        functools.partial(kernel, scale),
        out_shape=(out, out, out),
        in_specs=[pl.BlockSpec(memory_space=pl.ANY)] * 8,
        out_specs=[pl.BlockSpec(memory_space=pl.ANY)] * 3,
        scratch_shapes=[
            pltpu.VMEM((4, 2, ALL, DH), BF16),
            pltpu.VMEM((2, ALL, 128), F32),
            pltpu.VMEM((2, ALL), F32),
            pltpu.VMEM((NY, 8, CHUNK), F32),
            pltpu.VMEM((NY, 8, CHUNK), F32),
            pltpu.VMEM((NX, 8, CHUNK), F32),
            pltpu.VMEM((NZ, 3, EIGHTH, DH), BF16),
            pltpu.VMEM((2, 3 * DH, DH), BF16),
            pltpu.VMEM((2, 2, 3 * DH, DH), F32),
            pltpu.VMEM((2, 2, 3 * DH, DH), BF16),
            pltpu.VMEM((2, 2, 3, NX - 1, PART, DH), BF16),
            pltpu.VMEM((2, 2, 3, PART, DH), F32),
            pltpu.VMEM((2, 2, 3, PART, DH), BF16),
            pltpu.VMEM((2, 2, 3, NZ - 1, ZROWS, ZCOLS), BF16),
            pltpu.VMEM((2, 2, 3 * DH, DH), BF16),
            pltpu.VMEM((2, ALL, DH), F32),
            pltpu.VMEM((2, ALL, DH), F32),
            pltpu.VMEM((2, ALL, DH), F32),
            pltpu.VMEM((2, ALL, DH), BF16),
            pltpu.VMEM((2, ALL, DH), BF16),
            pltpu.VMEM((2, ALL, DH), BF16),
            pltpu.VMEM((2, ALL, DH), BF16),
            pltpu.VMEM((3, 2, ALL, DH), BF16),
            dma((4, 2)), dma((4, 2, NY)), dma((4, 2)), dma((2, 3)), dma,
            dma, dma, dma, dma, dma, dma, dma, dma,
            dma((2, 2, 3)), dma((2, 2, 3)), dma((2, 2, 3)), dma((2, 2, 3)),
            dma((2, 2, 3)), dma((2, 2, 3)), dma((2, 2, 3)), dma((2, 2, 3)),
            dma((3, 2)), dma((3, 2)), dma((3, 2)),
        ],
        compiler_params=pltpu.CompilerParams(
            collective_id=0, has_side_effects=True, vmem_limit_bytes=60 << 20
        ),
    )(queries, key_tokens, values, out_grad, learn_rates.T, w_gate, w_up, w_down)


def solution(mesh):
    tokens = P(("tok", "head"), None)
    heads = P("head", None, None)
    return jax.shard_map(
        body,
        mesh=mesh,
        in_specs=(tokens, tokens, tokens, tokens, P("tok", "head"), heads, heads, heads),
        out_specs=(tokens, tokens, tokens),
        check_vma=False,
    )
```

time: 111 us -> 97.7 us (0.88)
  Pallas kernels: 103 us -> 91.8 us
  local copies, waits for them, and re-layouts: 6.1 us -> 4.95 us
    pallas_call x1, Pallas kernels: 103 us -> 91.8 us  [body(): pl.pallas_call(functools.partial(kernel, scale), out_shape=(out, out, out...]
    unnamed x12 -> x7, local copies, waits for them, and re-layouts: 6.1 us -> 4.95 us
where the time goes in v2:
time: 97.7 us; the launch traced here: 97.4 us
  Pallas kernels  91.8 us (94%)
  local copies, waits for them, and re-layouts  4.95 us (5%)
    pallas_call x1, Pallas kernels, body(): pl.pallas_call(functools.partial(kernel, scale), out_shape=(out, out, out...  91.8 us
    unnamed x7, local copies, waits for them, and re-layouts  4.95 us

profile of v2, /device:TPU:1, one launch (start us, length us, event | category | flops | bytes accessed | tf_op | source)
XLA Modules:
  0.0 97.4 jit_solution(13096758106590167777)
XLA Ops:
  0.6 91.8 %shard_map.103 = (bf16[128,4096]{1,0:T(8,128)(2,1)}, bf16[128,4096]{1,0:T(8,128)(2,1)}, bf16[128,4096]{1,0:T(8,128)(2,1)}) custom-call(bf16[128,4096]{1,0:T(8,128)(2,1)} %q_in.1, bf16[128,4096]{1,0:T(8,128)(2,1)} %k_in.1, bf16[128,4096]{1,0:T(8,128)(2,1)} %v_in.1, bf16[128,4096]{1,0:T(8,128)(2,1)} %o_in.1, f32[2,1024]{1,0:T(2,128)} %bitcast.1, ...), custom_call_target="tpu_custom_call" | custom-call | tf_op jit(solution)/shard_map/pallas_call | solution.py:470
  92.5 0.0 copy-start.1
  92.5 2.4 %copy.14 = bf16[128,4096]{1,0:T(8,128)(2,1)} copy(bf16[128,4096]{1,0:T(8,128)(2,1)} %get-tuple-element.6) | data formatting | bytes 2097152
  94.8 0.0 copy-done.1
  94.8 0.0 copy-start
  94.8 1.0 copy.15
  95.8 0.6 copy-done
  96.4 1.0 copy.16
Async XLA Ops:
  92.5 2.4 %copy-start.1 = (bf16[128,4096]{1,0:T(8,128)(2,1)S(1)}, bf16[128,4096]{1,0:T(8,128)(2,1)}, u32[]{:S(2)}) copy-start(bf16[128,4096]{1,0:T(8,128)(2,1)} %get-tuple-element.7) | copy-start | bytes 3145732
  94.8 1.6 %copy-start = (bf16[128,4096]{1,0:T(8,128)(2,1)S(1)}, bf16[128,4096]{1,0:T(8,128)(2,1)}, u32[]{:S(2)}) copy-start(bf16[128,4096]{1,0:T(8,128)(2,1)} %get-tuple-element.8) | copy-start | bytes 3145732

commit v3 on v2

--- a/solution.py
+++ b/solution.py
@@ -332,28 +332,21 @@
         return cc, pl.ds(pl.multiple_of(cc * CHUNK, CHUNK), CHUNK)
 
     def query_side(h):
-        acc[1, h] = jnp.zeros((3 * DH, DH), F32)
-
-        def step(j, carry):
-            yy, rows = chunk_of(h, j)
-            qr = buf[2, h, rows]
-            orr = buf[3, h, rows]
-            ng = full[0, h, 0:DH]
-            nu = full[0, h, DH:2 * DH]
-            gp = mm(qr, ng)
-            up = mm(qr, nu)
-            qd = mm_rt(orr, full[0, h, 2 * DH:3 * DH])
-            s, act, rest, slope = silu_parts(gp)
-            hd = (act * up).astype(BF16)
-            dg = (qd * up * slope).astype(BF16)
-            du = (qd * act).astype(BF16)
-            stage[0, h, rows] = (mm_rt(dg, ng) + mm_rt(du, nu)).astype(BF16)
-            acc[1, h, 0:DH] += mm_lt(qr, dg)
-            acc[1, h, DH:2 * DH] += mm_lt(qr, du)
-            acc[1, h, 2 * DH:3 * DH] += mm_lt(hd, orr)
-            return carry
-
-        lax.fori_loop(0, NY, step, 0)
+        qr = buf[2, h]
+        orr = buf[3, h]
+        ng = full[0, h, 0:DH]
+        nu = full[0, h, DH:2 * DH]
+        gp = mm(qr, ng)
+        up = mm(qr, nu)
+        qd = mm_rt(orr, full[0, h, 2 * DH:3 * DH])
+        s, act, rest, slope = silu_parts(gp)
+        hd = (act * up).astype(BF16)
+        dg = (qd * up * slope).astype(BF16)
+        du = (qd * act).astype(BF16)
+        acc[1, h, 0:DH] = mm_lt(qr, dg)
+        acc[1, h, DH:2 * DH] = mm_lt(qr, du)
+        acc[1, h, 2 * DH:3 * DH] = mm_lt(hd, orr)
+        stage[0, h] = (mm_rt(dg, ng) + mm_rt(du, nu)).astype(BF16)
 
     def back(h, j):
         yy, rows = chunk_of(h, j)
@@ -376,15 +369,16 @@
         kg = mm_rt(dgate[h, rows], ag) + mm_rt(dup[h, rows], au)
         kg = kg + mm_rt(bg, w[h, 0:DH]) + mm_rt(bu, w[h, DH:2 * DH])
         stage[1, h, rows] = kg.astype(BF16)
-        send_out(1, h, yy, j == NY - 1)
         vg = mm(hid[h, rows], ad) + mm(bdh, w[h, 2 * DH:3 * DH])
         stage[2, h, rows] = (rates(h, rows) * vg).astype(BF16)
-        send_out(2, h, yy, j == NY - 1)
+        return yy
 
     def key_back():
         def step(j, carry):
-            back(0, j)
-            back(1, j)
+            spots_of = (back(0, j), back(1, j))
+            for a in (1, 2):
+                for h in range(2):
+                    send_out(a, h, spots_of[h], j == NY - 1)
             return carry
 
         lax.fori_loop(0, NY, step, 0)

time: 97.7 us -> 95 us (0.972)
  Pallas kernels: 91.8 us -> 89.2 us
    pallas_call x1, Pallas kernels: 91.8 us -> 89.2 us  [body(): pl.pallas_call(functools.partial(kernel, scale), out_shape=(out, out, out...]
where the time goes in v3:
time: 95 us; the launch traced here: 94.8 us
  Pallas kernels  89.2 us (94%)
  local copies, waits for them, and re-layouts  4.95 us (5%)
    pallas_call x1, Pallas kernels, body(): pl.pallas_call(functools.partial(kernel, scale), out_shape=(out, out, out...  89.2 us
    unnamed x7, local copies, waits for them, and re-layouts  4.95 us

profile of v3, /device:TPU:1, one launch (start us, length us, event | category | flops | bytes accessed | tf_op | source)
XLA Modules:
  0.0 94.8 jit_solution(12924398828115498421)
XLA Ops:
  0.6 89.2 %shard_map.103 = (bf16[128,4096]{1,0:T(8,128)(2,1)}, bf16[128,4096]{1,0:T(8,128)(2,1)}, bf16[128,4096]{1,0:T(8,128)(2,1)}) custom-call(bf16[128,4096]{1,0:T(8,128)(2,1)} %q_in.1, bf16[128,4096]{1,0:T(8,128)(2,1)} %k_in.1, bf16[128,4096]{1,0:T(8,128)(2,1)} %v_in.1, bf16[128,4096]{1,0:T(8,128)(2,1)} %o_in.1, f32[2,1024]{1,0:T(2,128)} %bitcast.1, ...), custom_call_target="tpu_custom_call" | custom-call | tf_op jit(solution)/shard_map/pallas_call | solution.py:464
  89.8 0.0 copy-start.1
  89.8 2.4 %copy.14 = bf16[128,4096]{1,0:T(8,128)(2,1)} copy(bf16[128,4096]{1,0:T(8,128)(2,1)} %get-tuple-element.6) | data formatting | bytes 2097152
  92.2 0.0 copy-done.1
  92.2 0.0 copy-start
  92.2 1.0 %copy.15 = bf16[128,4096]{1,0:T(8,128)(2,1)} copy(bf16[128,4096]{1,0:T(8,128)(2,1)S(1)} %copy-done.1) | data formatting | bytes 2097152
  93.2 0.6 copy-done
  93.8 1.0 %copy.16 = bf16[128,4096]{1,0:T(8,128)(2,1)} copy(bf16[128,4096]{1,0:T(8,128)(2,1)S(1)} %copy-done) | data formatting | bytes 2097152
Async XLA Ops:
  89.8 2.4 %copy-start.1 = (bf16[128,4096]{1,0:T(8,128)(2,1)S(1)}, bf16[128,4096]{1,0:T(8,128)(2,1)}, u32[]{:S(2)}) copy-start(bf16[128,4096]{1,0:T(8,128)(2,1)} %get-tuple-element.7) | copy-start | bytes 3145732
  92.2 1.6 %copy-start = (bf16[128,4096]{1,0:T(8,128)(2,1)S(1)}, bf16[128,4096]{1,0:T(8,128)(2,1)}, u32[]{:S(2)}) copy-start(bf16[128,4096]{1,0:T(8,128)(2,1)} %get-tuple-element.8) | copy-start | bytes 3145732

commit v4 on v3

--- a/solution.py
+++ b/solution.py
@@ -407,11 +407,11 @@
     key_forward(0, 2)
     for m in range(3):
         rs_x_start(0, 0, m)
-    send_in(2, 1)
-    send_in(3, 1)
     key_forward(1, 2)
     for m in range(3):
         rs_x_start(0, 1, m)
+    send_in(2, 1)
+    send_in(3, 1)
     send_in(2, 0)
     send_in(3, 0)
     for step in (rs_x_finish, rs_z_finish, ag_z_finish):

time: 95 us -> 95 us (level)
  no operation moved by 1% of the time
where the time goes in v4:
time: 95 us; the launch traced here: 94.8 us
  Pallas kernels  89.2 us (94%)
  local copies, waits for them, and re-layouts  4.95 us (5%)
    pallas_call x1, Pallas kernels, body(): pl.pallas_call(functools.partial(kernel, scale), out_shape=(out, out, out...  89.2 us
    unnamed x7, local copies, waits for them, and re-layouts  4.95 us

profile of v4, /device:TPU:1, one launch (start us, length us, event | category | flops | bytes accessed | tf_op | source)
XLA Modules:
  0.0 94.8 jit_solution(5053696676238719744)
XLA Ops:
  0.6 89.2 %shard_map.103 = (bf16[128,4096]{1,0:T(8,128)(2,1)}, bf16[128,4096]{1,0:T(8,128)(2,1)}, bf16[128,4096]{1,0:T(8,128)(2,1)}) custom-call(bf16[128,4096]{1,0:T(8,128)(2,1)} %q_in.1, bf16[128,4096]{1,0:T(8,128)(2,1)} %k_in.1, bf16[128,4096]{1,0:T(8,128)(2,1)} %v_in.1, bf16[128,4096]{1,0:T(8,128)(2,1)} %o_in.1, f32[2,1024]{1,0:T(2,128)} %bitcast.1, ...), custom_call_target="tpu_custom_call" | custom-call | tf_op jit(solution)/shard_map/pallas_call | solution.py:464
  89.8 0.0 copy-start.1
  89.8 2.4 %copy.14 = bf16[128,4096]{1,0:T(8,128)(2,1)} copy(bf16[128,4096]{1,0:T(8,128)(2,1)} %get-tuple-element.6) | data formatting | bytes 2097152
  92.2 0.0 copy-done.1
  92.2 0.0 copy-start
  92.2 1.0 %copy.15 = bf16[128,4096]{1,0:T(8,128)(2,1)} copy(bf16[128,4096]{1,0:T(8,128)(2,1)S(1)} %copy-done.1) | data formatting | bytes 2097152
  93.2 0.6 copy-done
  93.8 1.0 %copy.16 = bf16[128,4096]{1,0:T(8,128)(2,1)} copy(bf16[128,4096]{1,0:T(8,128)(2,1)S(1)} %copy-done) | data formatting | bytes 2097152
Async XLA Ops:
  89.8 2.4 %copy-start.1 = (bf16[128,4096]{1,0:T(8,128)(2,1)S(1)}, bf16[128,4096]{1,0:T(8,128)(2,1)}, u32[]{:S(2)}) copy-start(bf16[128,4096]{1,0:T(8,128)(2,1)} %get-tuple-element.7) | copy-start | bytes 3145732
  92.2 1.6 %copy-start = (bf16[128,4096]{1,0:T(8,128)(2,1)S(1)}, bf16[128,4096]{1,0:T(8,128)(2,1)}, u32[]{:S(2)}) copy-start(bf16[128,4096]{1,0:T(8,128)(2,1)} %get-tuple-element.8) | copy-start | bytes 3145732
